TPU v7x, 32 devices: a whole 2x2x4 slice. The times are simulated.
32 devices in a mesh: group: 2 (over y), walker: 4 (over z), param: 4 (over x, core).
Axes of the slice: x: 2, y: 2, z: 4, core: 2. Of those that a mesh axis runs over, the one named last changes fastest.
Arguments:
- activations: bfloat16 [96, 1024, 256], P(('group', 'walker'), 'param'), parts along dimension 0, may hold values from -6 to 6
- cotangents: bfloat16 [96, 1024, 1024], P(('group', 'walker'), 'param'), parts along dimension 0, may hold values from -0.0010036526 to 0.0010036526
- local_energy: float32 [96], P(('group', 'walker')), parts along dimension 0, may hold values from -6 to 6
- walker_ids: int32 [96], P(('group', 'walker')), parts along dimension 0, may hold values from 0 to 47, each once
- prev_direction: float32 [512, 1024], P('group', 'param'), parts along dimension 0, may hold values from -6 to 6
- column_order: int32 [2048], P('group'), parts along dimension 0, may hold values from 0 to 1023, each once
- weights: float32 [512, 1024], P('group', 'param'), parts along dimension 0, may hold values from -0.375 to 0.375
Outputs:
- direction: float32 [512, 1024], P('group', 'param'), parts along dimension 0
- new_weights: float32 [512, 1024], P('group', 'param'), parts along dimension 0
- coefficients: float32 [96], P(('group', 'walker')), parts along dimension 0
There are 2 independent parts, one for each index of `group`. A program takes and returns all parts, laid end to end along the dimension named above; each array names one. Nothing has to cross between parts.
Inputs may be any that keep to these rules, and one draw needn't show every extreme that they name: `walker_ids`: each walker id appears once. `column_order`: each column appears once.
All inputs are finite; a program needn't handle non-finite values.
Results may differ from a plain program's by a relative error of at most 0.0015.
Values may be sent and summed in bfloat16 or wider, within the bound.
A program may use at most 128 MiB of HBM per device.

v0:
```python
import jax
import jax.numpy as jnp
from jax import lax
from jax.sharding import PartitionSpec as P


def solve_system(system, zeta):
    factor = jnp.linalg.cholesky(system)
    column = zeta[:, None]
    middle = lax.linalg.triangular_solve(
        factor, column, left_side=True, lower=True, transpose_a=False
    )
    result = lax.linalg.triangular_solve(
        factor, middle, left_side=True, lower=True, transpose_a=True
    )
    return result[:, 0]


def shards(
    activations, cotangents, local_energy, walker_ids, prev_direction, column_order, weights
):
    rows = cotangents.shape[0]
    orb_local = cotangents.shape[1]
    width_in = activations.shape[2]
    walkers = rows * lax.axis_size("walker")
    walker_pos = lax.axis_index("walker")
    param_pos = lax.axis_index("param")
    grads = jnp.einsum(
        "wnd,won->wdo",
        lax.all_gather(activations, "param", axis=1, tiled=True),
        cotangents,
        preferred_element_type=jnp.float32,
    )
    flat = grads.reshape(rows, width_in * orb_local)
    column_total = lax.psum(jnp.sum(flat, axis=0), "walker")
    centered = (flat - column_total / walkers).astype(jnp.bfloat16)
    energies_all = lax.all_gather(local_energy, "walker", axis=0, tiled=True)
    energy_mean = jnp.mean(energies_all)
    centered_energy = energies_all[walker_ids] - energy_mean
    stored = lax.all_gather(prev_direction, "param", axis=1, tiled=True)
    my_order = lax.dynamic_slice_in_dim(column_order, param_pos * orb_local, orb_local)
    aligned = jnp.take(stored, my_order, axis=1)
    wide = centered.astype(jnp.float32)
    proj_part = jnp.dot(wide, aligned.reshape(-1), precision=lax.Precision.HIGHEST)
    block = lax.dot_general(
        centered,
        lax.all_gather(centered, "walker", axis=0, tiled=True),
        (((1,), (1,)), ((), ())),
        preferred_element_type=jnp.float32,
    )
    gram_mine, proj_mine = lax.psum((block, proj_part), "param")
    zeta_mine = centered_energy - 0.9 * proj_mine
    gram, zeta = (
        lax.all_gather(gram_mine, "walker", axis=0, tiled=True),
        lax.all_gather(zeta_mine, "walker", axis=0, tiled=True),
    )
    system = gram + 0.002 * jnp.eye(walkers, dtype=jnp.float32) + 1.0 / walkers
    solved = solve_system(system, zeta)
    mine = lax.dynamic_slice_in_dim(solved, walker_pos * rows, rows)
    update_part = jnp.dot(mine, wide, precision=lax.Precision.HIGHEST)
    update_total = lax.psum(update_part, "walker")
    direction = update_total.reshape(width_in, orb_local) + 0.9 * aligned
    return (direction, weights - 0.05 * direction, mine)


def solution(mesh):
    in_specs = (
        P(("group", "walker"), "param", None),
        P(("group", "walker"), "param", None),
        P(("group", "walker")),
        P(("group", "walker")),
        P("group", "param"),
        P("group"),
        P("group", "param"),
    )
    out_specs = (P("group", "param"), P("group", "param"), P(("group", "walker")))
    return jax.shard_map(shards, mesh=mesh, in_specs=in_specs, out_specs=out_specs, check_vma=False)
```

profile of v0, /device:TPU:0, one launch (start us, length us, event | category | flops | bytes accessed | tf_op | source)
XLA Modules:
  0.0 368.5 jit_solution(4993338365333594377)
XLA Ops:
  7.2 2.6 copy.23
  9.9 50.0 %all-gather.6.cloned.1.call-done = bf16[12,1024,256]{1,2,0:T(8,128)(2,1)} async-done(((bf16[12,256,256]{1,2,0:T(8,128)(2,1)}), bf16[12,1024,256]{1,2,0:T(8,128)(2,1)}) %all-gather.6.cloned.1.call-update) | async-done | bytes 6291472 | tf_op jit(solution)/shard_map/all_gather | solution.py:30
  59.9 6.5 %fusion.16 = (f32[256,256]{1,0:T(8,128)S(1)}, f32[12,256,256]{2,1,0:T(8,128)S(1)}) fusion(bf16[12,1024,256]{1,2,0:T(8,128)(2,1)} %all-gather.6.cloned.1.call-done, bf16[12,256,1024]{2,1,0:T(8,128)(2,1)} %param.8), kind=kOutput, calls=%fused_computation.36 | convolution fusion | flops 1611333632 | bytes 15990784 | tf_op jit(solution)/shard_map/wnd,won->wdo/dot_general | solution.py:28
  66.3 0.8 copy.33
  67.3 0.8 copy.25
  68.6 4.4 %copy.32 = f32[2,8,256,256]{3,1,2,0:T(8,128)} copy(f32[2,8,256,256]{3,2,1,0:T(8,128)S(1)} %bitcast.53) | data formatting | bytes 8388608
  73.0 29.6 %all-reduce.6.cloned.1.call-done = f32[65536]{0:T(1024)} async-done(((f32[65536]{0:T(1024)}), f32[65536]{0:T(1024)}) %all-reduce.6.cloned.1.call-update) | async-done | bytes 262160 | tf_op jit(solution)/shard_map/psum | solution.py:35
  102.7 1.0 broadcast_multiply_fusion
  103.7 3.9 %fusion.6 = bf16[1,12,65536]{2,1,0:T(8,128)(2,1)} fusion(f32[12,65536]{1,0:T(8,128)} %bitcast.51, f32[65536]{0:T(1024)S(1)} %broadcast_multiply_fusion), kind=kLoop, calls=%fused_computation.10 | loop fusion | flops 1572864 | bytes 4980736
  109.2 10.7 %all-reduce = f32[48]{0:T(128)S(1)} all-reduce(f32[48]{0:T(128)S(1)} %dynamic-update-slice.3), channel_id=1, replica_groups=mesh['group'=2,'walker'=4,'param'=4] {'walker'}, use_global_device_ids=true, to_apply=%add | all-reduce | flops 48 | bytes 384
  121.8 0.8 compare_and_fusion
  122.7 2.9 gather_fusion.1
  125.5 1.8 select_bitcast_fusion
  127.3 1.8 copy.31
  129.1 0.8 sub.32
  129.9 1.3 subtract_convert_fusion.1
  131.4 1.2 copy.34
  132.6 3.1 fusion.2
  135.7 136.8 %all-gather.10.cloned.1.call-done = bf16[4,12,65536]{2,1,0:T(8,128)(2,1)} async-done(((bf16[1,12,65536]{2,1,0:T(8,128)(2,1)}), bf16[4,12,65536]{2,1,0:T(8,128)(2,1)}) %all-gather.10.cloned.1.call-update) | async-done | bytes 6291472 | tf_op jit(solution)/shard_map/all_gather | solution.py:47
  272.6 6.0 %reshape.79 = bf16[48,65536]{1,0:T(8,128)(2,1)} reshape(bf16[4,12,65536]{2,1,0:T(8,128)(2,1)} %all-gather.10.cloned.1.call-done) | data formatting | bytes 12582912
  278.6 5.8 %fusion.5 = f32[12,48]{1,0:T(8,128)S(1)} fusion(bf16[48,65536]{1,0:T(8,128)(2,1)} %reshape.79, f32[12,65536]{1,0:T(8,128)} %bitcast.52, f32[65536]{0:T(1024)S(1)} %broadcast_multiply_fusion), kind=kOutput, calls=%fused_computation.9 | convolution fusion | flops 77070336 | bytes 9701632 | tf_op jit(solution)/shard_map/dot_general | solution.py:45
  284.4 7.2 %all-reduce.2 = (f32[12,48]{1,0:T(8,128)S(1)}, f32[12]{0:T(128)S(1)}) all-reduce(f32[12,48]{1,0:T(8,128)S(1)} %fusion.5, f32[12]{0:T(128)S(1)} %fusion.2), channel_id=1, replica_groups=mesh['group'=2,'walker'=4,'param'=4] {'param'}, use_global_device_ids=true, to_apply=%region_2.0 | all-reduce | flops 588 | bytes 4704 | tf_op jit(solution)/shard_map/psum | solution.py:51
  291.6 13.1 %all-gather.1 = f32[4,12,48]{2,1,0:T(8,128)S(1)} all-gather(f32[1,12,48]{2,1,0:T(8,128)S(1)} %bitcast.59), channel_id=1, replica_groups=mesh['group'=2,'walker'=4,'param'=4] {'walker'}, dimensions={0}, use_global_device_ids=true | all-gather | bytes 11520 | tf_op jit(solution)/shard_map/all_gather | solution.py:54
  304.8 4.4 %cholesky.16 = f32[48,48]{1,0:T(8,128)S(1)} custom-call(f32[48,48]{1,0:T(8,128)S(1)} %fusion.11), custom_call_target="Cholesky" | custom-call | tf_op jit(solution)/shard_map/jit(cholesky)/cholesky | solution.py:8
  310.6 3.7 custom-call.8
  314.3 8.9 %all-reduce.1 = f32[48]{0:T(128)S(1)} all-reduce(f32[48]{0:T(128)S(1)} %subtract_dynamic-update-slice_fusion), channel_id=1, replica_groups=mesh['group'=2,'walker'=4,'param'=4] {'walker'}, use_global_device_ids=true, to_apply=%add.1 | all-reduce | flops 48 | bytes 384
  323.6 1.0 fusion.12
  324.7 0.8 copy.26
  325.7 33.5 %all-reduce.8.cloned.1.call-done = f32[256,256]{0,1:T(8,128)} async-done(((f32[256,256]{0,1:T(8,128)}), f32[256,256]{0,1:T(8,128)}) %all-reduce.8.cloned.1.call-update) | async-done | bytes 262160 | tf_op jit(solution)/shard_map/psum | solution.py:61
  359.2 1.1 multiply_subtract_fusion
  360.3 0.8 copy.28
  361.1 0.8 copy.29
  (51 shorter events, 5.2 us)
Async XLA Ops:
  7.2 52.7 %all-gather.6.cloned.1.call-start = ((), (), s32[]{:S(2)}) async-start(), calls=%async_computation | async-start | bytes 7864320 | tf_op jit(solution)/shard_map/all_gather | solution.py:30
  9.8 57.4 %copy-start.1 = (f32[256,256]{1,0:T(8,128)S(1)}, f32[256,256]{1,0:T(8,128)}, u32[]{:S(2)}) copy-start(f32[256,256]{1,0:T(8,128)} %param.11) | copy-start | bytes 786436
  9.8 92.9 %all-reduce.6.cloned.1.call-start = ((), (), s32[]{:S(2)}) async-start(), calls=%async_computation.1 | async-start | bytes 524288 | tf_op jit(solution)/shard_map/psum | solution.py:35
  67.2 55.4 %all-gather.8.cloned.1.call-start = ((), (), s32[]{:S(2)}) async-start(), calls=%async_computation.2 | async-start | bytes 1310720 | tf_op jit(solution)/shard_map/all_gather | solution.py:40
  68.1 204.4 %all-gather.10.cloned.1.call-start = ((), (), s32[]{:S(2)}) async-start(), calls=%async_computation.4 | async-start | bytes 10485760 | tf_op jit(solution)/shard_map/all_gather | solution.py:47
  103.7 4.0 %copy-start.7 = (u32[32]{0:T(128)S(1)}, u32[32]{0:T(128)}, u32[]{:S(2)}) copy-start(u32[32]{0:T(128)} %constant.99) | copy-start | bytes 388
  103.7 5.2 %copy-start.5 = (f32[12]{0:T(128)S(1)}, f32[12]{0:T(128)}, u32[]{:S(2)}) copy-start(f32[12]{0:T(128)} %param.9) | copy-start | bytes 148
  103.7 16.2 %copy-start.6 = (s32[12]{0:T(128)S(1)}, s32[12]{0:T(128)}, u32[]{:S(2)}) copy-start(s32[12]{0:T(128)} %param.10) | copy-start | bytes 148
  107.6 251.6 %all-reduce.8.cloned.1.call-start = ((), (), s32[]{:S(2)}) async-start(), calls=%async_computation.3 | async-start | bytes 524288 | tf_op jit(solution)/shard_map/psum | solution.py:61
  131.2 1.4 copy-start.3
  284.4 41.2 %copy-start.2 = (f32[256,256]{1,0:T(8,128)S(1)}, f32[256,256]{1,0:T(8,128)}, u32[]{:S(2)}) copy-start(f32[256,256]{1,0:T(8,128)} %param.13) | copy-start | bytes 786436
  284.4 74.8 %copy-start = (f32[256,256]{1,0:T(8,128)S(1)}, f32[256,256]{1,0:T(8,128)}, u32[]{:S(2)}) copy-start(f32[256,256]{1,0:T(8,128)} %gather_fusion.1) | copy-start | bytes 786436
  323.6 38.3 %copy-start.4 = (f32[12]{0:T(128)}, f32[12]{0:T(128)S(1)}, u32[]{:S(2)}) copy-start(f32[12]{0:T(128)S(1)} %dynamic_slice.7) | copy-start | bytes 148
Sparse Core Ops, SparseCore 0:
  9.9 49.8 all-gather.5
  67.3 35.3 all-reduce.5
  104.9 16.4 all-gather.7
  122.9 149.6 all-gather.9
  325.7 33.4 all-reduce.7
where the time goes:
time: 369 us; the launch traced here: 368 us
  waiting for transfers between devices  250 us (68%)
  blocking collectives  40 us (11%)
  local copies, waits for them, and re-layouts  26.4 us (7%)
  other arithmetic  19.9 us (5%)
  matrix products  16.6 us (4%)
  between operations  15.3 us (4%)
    all_gather x1, waiting for transfers between devices, shards(): lax.all_gather(centered, 'walker', axis=0, tiled=True)  137 us
    all_gather x1, waiting for transfers between devices, shards(): lax.all_gather(activations, 'param', axis=1, tiled=True)  50 us
    psum x1, waiting for transfers between devices, shards(): update_total = lax.psum(update_part, 'walker')  33.5 us
    psum x1, waiting for transfers between devices, shards(): column_total = lax.psum(jnp.sum(flat, axis=0), 'walker')  29.6 us
    unnamed x2, blocking collectives  19.6 us
    unnamed x32, local copies, waits for them, and re-layouts  19.2 us
    all_gather x1, blocking collectives, shards(): lax.all_gather(gram_mine, 'walker', axis=0, tiled=True)  13.1 us
  transfers between devices with their start and end apart: 5, of which 4 were waited for; matrix products, arithmetic and copies ran while one was open for 7% of the time, Pallas kernels for 0%

commit v1 on v0

--- a/solution.py
+++ b/solution.py
@@ -2,6 +2,24 @@
 import jax.numpy as jnp
 from jax import lax
 from jax.sharding import PartitionSpec as P
+from jax.lax import axis_size, ppermute
+
+
+def _switch_sides(piece_in, along_axis):
+    world_n = axis_size(along_axis)
+
+    def _save_lines(piece_out, w2):
+        if w2 >= world_n:
+            return piece_out
+        built = _save_lines(
+            piece_out
+            + ppermute(piece_out, along_axis, [(to_i, to_i ^ w2) for to_i in range(world_n)]),
+            2 * w2,
+        )
+        return built
+
+    plain = _save_lines(piece_in, 1)
+    return plain
 
 
 def solve_system(system, zeta):
@@ -58,7 +76,7 @@
     solved = solve_system(system, zeta)
     mine = lax.dynamic_slice_in_dim(solved, walker_pos * rows, rows)
     update_part = jnp.dot(mine, wide, precision=lax.Precision.HIGHEST)
-    update_total = lax.psum(update_part, "walker")
+    update_total = _switch_sides(update_part, "walker")
     direction = update_total.reshape(width_in, orb_local) + 0.9 * aligned
     return (direction, weights - 0.05 * direction, mine)
 

time: 369 us -> 352 us (0.954)
  waiting for transfers between devices: 250 us -> 231 us
    psum x1 -> x0, waiting for transfers between devices: 33.5 us -> none  [shards(): update_total = lax.psum(update_part, 'walker')]
    ppermute x0 -> x2, waiting for transfers between devices: none -> 14.3 us  [_save_lines(): ppermute(piece_out, along_axis, [(to_i, to_i ^ w2) for to_i in range(worl...]
    unnamed x32 -> x30, local copies, waits for them, and re-layouts: 19.2 us -> 20.1 us
  transfers between devices with their start and end apart: 5 -> 6, of which waited for: 4 -> 5; matrix products, arithmetic and copies ran while one was open for 7% -> 8% of each run, Pallas kernels for 0% -> 0%
where the time goes in v1:
time: 352 us; the launch traced here: 351 us
  waiting for transfers between devices  231 us (66%)
  blocking collectives  40.1 us (11%)
  local copies, waits for them, and re-layouts  26.6 us (8%)
  other arithmetic  19 us (5%)
  matrix products  16.6 us (5%)
  between operations  15.3 us (4%)
    all_gather x1, waiting for transfers between devices, shards(): lax.all_gather(centered, 'walker', axis=0, tiled=True)  137 us
    all_gather x1, waiting for transfers between devices, shards(): lax.all_gather(activations, 'param', axis=1, tiled=True)  50 us
    psum x1, waiting for transfers between devices, shards(): column_total = lax.psum(jnp.sum(flat, axis=0), 'walker')  29.7 us
    unnamed x30, local copies, waits for them, and re-layouts  20.1 us
    unnamed x2, blocking collectives  19.8 us
    ppermute x2, waiting for transfers between devices, _save_lines(): ppermute(piece_out, along_axis, [(to_i, to_i ^ w2) for to_i in range(worl...  14.3 us
    all_gather x1, blocking collectives, shards(): lax.all_gather(gram_mine, 'walker', axis=0, tiled=True)  13.1 us
    psum x1, blocking collectives, shards(): gram_mine, proj_mine = lax.psum((block, proj_part), 'param')  7.22 us
  transfers between devices with their start and end apart: 6, of which 5 were waited for; matrix products, arithmetic and copies ran while one was open for 8% of the time, Pallas kernels for 0%

profile of v1, /device:TPU:0, one launch (start us, length us, event | category | flops | bytes accessed | tf_op | source)
XLA Modules:
  0.0 351.3 jit_solution(11939411952838356240)
XLA Ops:
  7.2 2.6 copy.23
  9.9 50.0 %all-gather.6.cloned.1.call-done = bf16[12,1024,256]{1,2,0:T(8,128)(2,1)} async-done(((bf16[12,256,256]{1,2,0:T(8,128)(2,1)}), bf16[12,1024,256]{1,2,0:T(8,128)(2,1)}) %all-gather.6.cloned.1.call-update) | async-done | bytes 6291472 | tf_op jit(solution)/shard_map/all_gather | solution.py:48
  59.9 6.5 %fusion.16 = (f32[256,256]{1,0:T(8,128)S(1)}, f32[12,256,256]{2,1,0:T(8,128)S(1)}) fusion(bf16[12,1024,256]{1,2,0:T(8,128)(2,1)} %all-gather.6.cloned.1.call-done, bf16[12,256,1024]{2,1,0:T(8,128)(2,1)} %param.8), kind=kOutput, calls=%fused_computation.36 | convolution fusion | flops 1611333632 | bytes 15990784 | tf_op jit(solution)/shard_map/wnd,won->wdo/dot_general | solution.py:46
  66.3 0.8 copy.33
  67.3 0.8 copy.25
  68.6 4.4 %copy.32 = f32[2,8,256,256]{3,1,2,0:T(8,128)} copy(f32[2,8,256,256]{3,2,1,0:T(8,128)S(1)} %bitcast.53) | data formatting | bytes 8388608
  73.0 29.7 %all-reduce.5.cloned.1.call-done = f32[65536]{0:T(1024)} async-done(((f32[65536]{0:T(1024)}), f32[65536]{0:T(1024)}) %all-reduce.5.cloned.1.call-update) | async-done | bytes 262160 | tf_op jit(solution)/shard_map/psum | solution.py:53
  102.7 1.0 broadcast_multiply_fusion
  103.7 3.9 %fusion.6 = bf16[1,12,65536]{2,1,0:T(8,128)(2,1)} fusion(f32[12,65536]{1,0:T(8,128)} %bitcast.51, f32[65536]{0:T(1024)S(1)} %broadcast_multiply_fusion), kind=kLoop, calls=%fused_computation.10 | loop fusion | flops 1572864 | bytes 4980736
  109.1 10.7 %all-reduce = f32[48]{0:T(128)S(1)} all-reduce(f32[48]{0:T(128)S(1)} %dynamic-update-slice.3), channel_id=1, replica_groups=mesh['group'=2,'walker'=4,'param'=4] {'walker'}, use_global_device_ids=true, to_apply=%add | all-reduce | flops 48 | bytes 384
  122.6 2.9 gather_fusion.1
  125.5 1.8 select_bitcast_fusion
  127.3 1.8 copy.31
  129.8 1.3 subtract_convert_fusion.1
  131.3 1.2 copy.34
  132.5 3.1 fusion.2
  135.7 136.9 %all-gather.10.cloned.1.call-done = bf16[4,12,65536]{2,1,0:T(8,128)(2,1)} async-done(((bf16[1,12,65536]{2,1,0:T(8,128)(2,1)}), bf16[4,12,65536]{2,1,0:T(8,128)(2,1)}) %all-gather.10.cloned.1.call-update) | async-done | bytes 6291472 | tf_op jit(solution)/shard_map/all_gather | solution.py:65
  272.6 6.0 %reshape.79 = bf16[48,65536]{1,0:T(8,128)(2,1)} reshape(bf16[4,12,65536]{2,1,0:T(8,128)(2,1)} %all-gather.10.cloned.1.call-done) | data formatting | bytes 12582912
  278.6 5.8 %fusion.5 = f32[12,48]{1,0:T(8,128)S(1)} fusion(bf16[48,65536]{1,0:T(8,128)(2,1)} %reshape.79, f32[12,65536]{1,0:T(8,128)} %bitcast.52, f32[65536]{0:T(1024)S(1)} %broadcast_multiply_fusion), kind=kOutput, calls=%fused_computation.9 | convolution fusion | flops 77070336 | bytes 9701632 | tf_op jit(solution)/shard_map/dot_general | solution.py:63
  284.4 7.2 %all-reduce.2 = (f32[12,48]{1,0:T(8,128)S(1)}, f32[12]{0:T(128)S(1)}) all-reduce(f32[12,48]{1,0:T(8,128)S(1)} %fusion.5, f32[12]{0:T(128)S(1)} %fusion.2), channel_id=1, replica_groups=mesh['group'=2,'walker'=4,'param'=4] {'param'}, use_global_device_ids=true, to_apply=%region_2.0 | all-reduce | flops 588 | bytes 4704 | tf_op jit(solution)/shard_map/psum | solution.py:69
  291.6 13.1 %all-gather.1 = f32[4,12,48]{2,1,0:T(8,128)S(1)} all-gather(f32[1,12,48]{2,1,0:T(8,128)S(1)} %bitcast.60), channel_id=1, replica_groups=mesh['group'=2,'walker'=4,'param'=4] {'walker'}, dimensions={0}, use_global_device_ids=true | all-gather | bytes 11520 | tf_op jit(solution)/shard_map/all_gather | solution.py:72
  304.9 4.4 %cholesky.16 = f32[48,48]{1,0:T(8,128)S(1)} custom-call(f32[48,48]{1,0:T(8,128)S(1)} %fusion.11), custom_call_target="Cholesky" | custom-call | tf_op jit(solution)/shard_map/jit(cholesky)/cholesky | solution.py:26
  310.6 3.7 %custom-call.8 = f32[1,48,48]{1,2,0:T(8,128)S(1)} custom-call(f32[1,48,48]{2,1,0:T(8,128)S(1)} %fusion.8), custom_call_target="InvertDiagBlocksLowerTriangular" | custom-call | tf_op jit(solution)/shard_map/triangular_solve | solution.py:31
  314.3 9.0 %all-reduce.1 = f32[48]{0:T(128)S(1)} all-reduce(f32[48]{0:T(128)S(1)} %subtract_dynamic-update-slice_fusion), channel_id=1, replica_groups=mesh['group'=2,'walker'=4,'param'=4] {'walker'}, use_global_device_ids=true, to_apply=%add.1 | all-reduce | flops 48 | bytes 384
  323.7 1.0 fusion.12
  324.7 1.5 collective-permute-start
  326.2 6.6 %collective-permute-done = f32[65536]{0:T(1024)S(1)} collective-permute-done((f32[65536]{0:T(1024)S(1)}, f32[65536]{0:T(1024)S(1)}, u32[]{:S(2)}, u32[]{:S(2)}) %collective-permute-start) | collective-permute-done | bytes 262176 | tf_op jit(solution)/shard_map/ppermute | solution.py:16
  332.9 1.1 collective-permute-start.1
  333.9 1.1 copy.27
  335.0 7.6 %collective-permute-done.1 = f32[65536]{0:T(1024)S(1)} collective-permute-done((f32[65536]{0:T(1024)S(1)}, f32[65536]{0:T(1024)S(1)}, u32[]{:S(2)}, u32[]{:S(2)}) %collective-permute-start.1) | collective-permute-done | bytes 262176 | tf_op jit(solution)/shard_map/ppermute | solution.py:16
  343.1 0.8 copy.28
  343.9 0.8 copy.29
  (52 shorter events, 6.9 us)
Async XLA Ops:
  7.2 52.7 %all-gather.6.cloned.1.call-start = ((), (), s32[]{:S(2)}) async-start(), calls=%async_computation | async-start | bytes 7864320 | tf_op jit(solution)/shard_map/all_gather | solution.py:48
  9.8 57.4 %copy-start.1 = (f32[256,256]{1,0:T(8,128)S(1)}, f32[256,256]{1,0:T(8,128)}, u32[]{:S(2)}) copy-start(f32[256,256]{1,0:T(8,128)} %param.11) | copy-start | bytes 786436
  9.8 92.9 %all-reduce.5.cloned.1.call-start = ((), (), s32[]{:S(2)}) async-start(), calls=%async_computation.1 | async-start | bytes 524288 | tf_op jit(solution)/shard_map/psum | solution.py:53
  67.2 55.4 %all-gather.8.cloned.1.call-start = ((), (), s32[]{:S(2)}) async-start(), calls=%async_computation.2 | async-start | bytes 1310720 | tf_op jit(solution)/shard_map/all_gather | solution.py:58
  68.1 204.5 %all-gather.10.cloned.1.call-start = ((), (), s32[]{:S(2)}) async-start(), calls=%async_computation.3 | async-start | bytes 10485760 | tf_op jit(solution)/shard_map/all_gather | solution.py:65
  103.7 3.9 %copy-start.6 = (u32[32]{0:T(128)S(1)}, u32[32]{0:T(128)}, u32[]{:S(2)}) copy-start(u32[32]{0:T(128)} %constant.99) | copy-start | bytes 388
  103.7 5.2 %copy-start.4 = (f32[12]{0:T(128)S(1)}, f32[12]{0:T(128)}, u32[]{:S(2)}) copy-start(f32[12]{0:T(128)} %param.9) | copy-start | bytes 148
  103.7 16.2 %copy-start.5 = (s32[12]{0:T(128)S(1)}, s32[12]{0:T(128)}, u32[]{:S(2)}) copy-start(s32[12]{0:T(128)} %param.10) | copy-start | bytes 148
  131.1 1.4 copy-start.2
  284.4 58.5 %copy-start = (f32[256,256]{1,0:T(8,128)S(1)}, f32[256,256]{1,0:T(8,128)}, u32[]{:S(2)}) copy-start(f32[256,256]{1,0:T(8,128)} %gather_fusion.1) | copy-start | bytes 786436
  323.7 21.0 %copy-start.3 = (f32[12]{0:T(128)}, f32[12]{0:T(128)S(1)}, u32[]{:S(2)}) copy-start(f32[12]{0:T(128)S(1)} %dynamic_slice.7) | copy-start | bytes 148
  324.7 8.1 %collective-permute-start = (f32[65536]{0:T(1024)S(1)}, f32[65536]{0:T(1024)S(1)}, u32[]{:S(2)}, u32[]{:S(2)}) collective-permute-start(f32[65536]{0:T(1024)S(1)} %bitcast.56), channel_id=1, source_target_pairs={{0,4},{4,0},{8,12},{12,8},{1,5},{5,1},{9,13},{13,9},{2,6},{6,2},{1... | collective-permute-start | bytes 786440 | tf_op jit(solution)/shard_map/ppermute | solution.py:16
  332.9 9.8 %collective-permute-start.1 = (f32[65536]{0:T(1024)S(1)}, f32[65536]{0:T(1024)S(1)}, u32[]{:S(2)}, u32[]{:S(2)}) collective-permute-start(f32[65536]{0:T(1024)S(1)} %add.63), channel_id=1, source_target_pairs={{0,8},{4,12},{8,0},{12,4},{1,9},{5,13},{9,1},{13,5},{2,10},{6,14},... | collective-permute-start | bytes 786440 | tf_op jit(solution)/shard_map/ppermute | solution.py:16
Sparse Core Ops, SparseCore 0:
  9.9 49.8 all-gather.5
  67.3 35.3 all-reduce.4
  104.9 16.4 all-gather.7
  122.9 149.6 all-gather.9
